TPU v7x, 256 devices: a whole 4x4x8 slice. The times are simulated.
256 devices in a mesh: micro: 8 (over x, y_hi), macro: 32 (over z, y_lo, core).
Axes of the slice: x: 4, y: 4 (y_hi: 2, y_lo: 2; y = y_hi * 2 + y_lo), z: 8, core: 2. Of those that a mesh axis runs over, the one named last changes fastest.
Arguments:
- interaction: bfloat16 [32, 6, 1024, 6, 1024], P('macro', None, 'micro'), may hold values from -0.013671875 to 0.013671875
- cluster_moduli: float32 [32, 3, 1024], P('macro', None, 'micro'), may hold values from 0.5 to 2
- cluster_fraction: float32 [32, 1024], P('macro', 'micro'), may hold values from 0.1 to 10
- plastic_flag: int32 [32, 1024], P('macro', 'micro'), may hold values 0 or 1
- micro_id: int32 [2048, 1], P('macro'), may hold values from 0 to 31; in each aligned block of 64 rows (0 to 63, 64 to 127, ...) at most 6 rows name the same one
- macro_strain: float32 [2048, 6], P('macro'), may hold values from -6 to 6
- cluster_state: float32 [2048, 6, 1024], P('macro', None, 'micro'), may hold values from -4 to 4
Outputs:
- cluster_strain: float32 [2048, 6, 1024], P('macro', None, 'micro')
- hom_stress: float32 [6, 2048], P(None, 'macro')
- residual: float32 [3, 2048], P(None, 'macro')
Inputs may be any that keep to these rules, and one draw needn't show every extreme that they name: `micro_id`: in each aligned block of 64 points (one slab), no microstructure is named more than 6 times, and in some block one is named exactly 6 times.
All inputs are finite; a program needn't handle non-finite values. No bound on the sum of `plastic_flag` on one device may be relied on, other than what follows from the above.
Results may differ from a plain program's by a relative error of at most 0.00074.
Values may be sent and summed in bfloat16 or wider, within the bound.
A program may use at most 64 MiB of HBM per device.

v0:
```python
import jax
import jax.numpy as jnp
from jax import lax
from jax.sharding import PartitionSpec as P

ITERS = 3
GX = 8
GY = 8


LAM_REF = 1.0
MU_REF = 1.0


def with_halo(cells, sides, width):
    for axis, dim in sides:
        count = lax.axis_size(axis)
        ends = count - 1
        head = lax.slice_in_dim(cells, 0, width, axis=dim)
        tail = lax.slice_in_dim(cells, cells.shape[dim] - width, cells.shape[dim], axis=dim)
        cells = jnp.concatenate(
            [
                lax.ppermute(tail, axis, [(i, (i + 1) % count) for i in range(ends)]),
                cells,
                lax.ppermute(head, axis, [((i + 1) % count, i) for i in range(ends)]),
            ],
            axis=dim,
        )
    return cells


def stress_update(strain, moduli, plastic):
    lame_first = moduli[0]
    shear_mod = moduli[1]
    yield_level = moduli[2]
    volume_part = strain[:, 0] + strain[:, 1] + strain[:, 2]
    normal_dev = strain[:, 0:3] - volume_part[:, None] / 3.0
    shear_part = strain[:, 3:6]
    dev_square = jnp.sum(normal_dev * normal_dev, axis=1) + 2.0 * jnp.sum(
        shear_part * shear_part, axis=1
    )
    softening = 1.0 / jnp.sqrt(
        1.0 + 4.0 * shear_mod * shear_mod * dev_square / (yield_level * yield_level)
    )
    factor = 1.0 + plastic.astype(jnp.float32) * (softening - 1.0)
    bulk_stress = (lame_first + 2.0 * shear_mod / 3.0) * volume_part
    deviator = jnp.concatenate([normal_dev, shear_part], axis=1)
    scaled = 2.0 * (shear_mod * factor)[:, None] * deviator
    stress = jnp.concatenate([scaled[:, 0:3] + bulk_stress[:, None], scaled[:, 3:6]], axis=1)
    ref_normal = LAM_REF * volume_part[:, None] + 2.0 * MU_REF * strain[:, 0:3]
    ref_shear = 2.0 * MU_REF * strain[:, 3:6]
    reference_stress = jnp.concatenate([ref_normal, ref_shear], axis=1)
    return (stress, stress - reference_stress)


def central_diff(field, axis_number):
    widths = [(1, 1) if dim_number == axis_number else (0, 0) for dim_number in range(field.ndim)]
    padded = jnp.pad(field, widths)
    length = field.shape[axis_number]
    upper = lax.slice_in_dim(padded, 2, length + 2, axis=axis_number)
    lower = lax.slice_in_dim(padded, 0, length, axis=axis_number)
    return 0.5 * (upper - lower)


def local(
    interaction,
    cluster_moduli,
    cluster_fraction,
    plastic_flag,
    micro_id,
    macro_strain,
    cluster_state,
):
    holders = lax.axis_size("macro")
    points = micro_id.shape[0]
    capacity = 3 * points // holders
    bucket_count = holders * capacity
    local_width = cluster_state.shape[2]
    width = interaction.shape[4]
    owner_id = micro_id[:, 0]
    onehot = (owner_id[:, None] == jnp.arange(holders, dtype=jnp.int32)[None, :]).astype(jnp.int32)
    before = jnp.cumsum(onehot, axis=0) - onehot
    rank_slot = jnp.sum(before * onehot, axis=1)
    target_slot = owner_id * capacity + rank_slot
    chooser = (jnp.arange(bucket_count, dtype=jnp.int32)[:, None] == target_slot[None, :]).astype(
        jnp.float32
    )
    state_rows = cluster_state.reshape(points, 6 * local_width)
    bucket_state = jnp.dot(chooser, state_rows, precision=lax.Precision.HIGHEST).reshape(
        bucket_count, 6, local_width
    )
    bucket_target = jnp.dot(chooser, macro_strain, precision=lax.Precision.HIGHEST)
    strain, target = (
        lax.all_to_all(bucket_state, "macro", split_axis=0, concat_axis=0, tiled=True),
        lax.all_to_all(bucket_target, "macro", split_axis=0, concat_axis=0, tiled=True),
    )
    moduli = cluster_moduli[0]
    plastic = plastic_flag[0]
    fraction = cluster_fraction[0]
    coupling = interaction[0].reshape(6 * local_width, 6, width)
    contract = (((1, 2), (1, 2)), ((), ()))
    for iteration in range(ITERS):
        stress, polarization = stress_update(strain, moduli, plastic)
        polar_low = polarization.astype(jnp.bfloat16)
        gathered = lax.all_gather(polar_low, "micro", axis=2, tiled=True)
        coupled = lax.dot_general(gathered, coupling, contract, preferred_element_type=jnp.float32)
        strain = target[:, :, None] - coupled.reshape(bucket_count, 6, local_width)
    stress, polarization = stress_update(strain, moduli, plastic)
    weighted = jnp.sum(stress * fraction[None, None, :], axis=2)
    weight_total = jnp.sum(fraction)

    def to_home(values):
        flat_values = values.reshape(bucket_count, -1)
        return lax.dot_general(
            chooser, flat_values, (((0,), (0,)), ((), ())), precision=lax.Precision.HIGHEST
        )

    summed, total_weight = lax.psum((weighted, weight_total), "micro")
    averaged = summed / total_weight
    back_state, back_stress = (
        lax.all_to_all(strain, "macro", split_axis=0, concat_axis=0, tiled=True),
        lax.all_to_all(averaged, "macro", split_axis=0, concat_axis=0, tiled=True),
    )
    home_stress = to_home(back_stress)
    home_state = to_home(back_state).reshape(points, 6, local_width)
    hom_stress = home_stress.T
    planes = points // (GX * GY)
    grid = hom_stress.reshape(6, planes, GX, GY)
    along_x = central_diff(grid, 2)
    along_y = central_diff(grid, 3)
    padded_rim = with_halo(grid[2:5], (("macro", 1),), 1)
    along_z = 0.5 * (padded_rim[:, 2:] - padded_rim[:, :-2])
    res_x = along_x[0] + along_y[5] + along_z[2]
    res_y = along_x[5] + along_y[1] + along_z[1]
    res_z = along_x[4] + along_y[3] + along_z[0]
    residual = jnp.stack([res_x, res_y, res_z], axis=0).reshape(3, points)
    return (home_state, hom_stress, residual)


def solution(mesh):
    placed = (
        P("macro", None, "micro", None, None),
        P("macro", None, "micro"),
        P("macro", "micro"),
        P("macro", "micro"),
        P("macro", None),
        P("macro", None),
        P("macro", None, "micro"),
    )
    return jax.shard_map(
        local,
        mesh=mesh,
        in_specs=placed,
        out_specs=(P("macro", None, "micro"), P(None, "macro"), P(None, "macro")),
        check_vma=False,
    )
```

profile of v0, /device:TPU:1, one launch (start us, length us, event | category | flops | bytes accessed | tf_op | source)
XLA Modules:
  0.0 336.2 jit_solution(15428226062934434208)
XLA Ops:
  7.2 0.0 copy-start
  7.2 0.8 fusion.58
  8.0 0.1 reduce_window_sum.11
  8.1 0.8 select_reduce_fusion
  8.9 0.7 multiply_add_fusion.3
  9.6 0.5 fusion.46
  10.1 1.2 copy.26
  11.3 11.1 %all-to-all-start.1 = ((f32[192,6,128]{2,1,0:T(8,128)}), f32[192,6,128]{2,1,0:T(8,128)S(1)}, u32[]{:S(2)}, u32[]{:S(2)}) async-start(f32[192,6,128]{2,1,0:T(8,128)} %copy.26), calls=%async_computation.1 | async-start | bytes 1572864 | tf_op jit(solution)/shard_map/all_to_all | solution.py:94
  22.5 0.0 all-gather.4.cloned.1.call-start
  22.6 22.5 %all-to-all-done.1 = f32[192,6,128]{2,1,0:T(8,128)S(1)} async-done(((f32[192,6,128]{2,1,0:T(8,128)}), f32[192,6,128]{2,1,0:T(8,128)S(1)}, u32[]{:S(2)}, u32[]{:S(2)}) %all-to-all-start.1) | async-done | bytes 589856 | tf_op jit(solution)/shard_map/all_to_all | solution.py:94
  45.1 0.2 fusion.62
  45.4 0.2 fusion.61
  45.5 0.1 multiply_reduce_fusion.7
  45.7 0.0 copy-start.4
  45.8 0.8 fusion.42
  46.6 0.0 all-gather.4.cloned.1.call-update
  46.6 0.0 all-gather.6.cloned.1.call-start
  46.7 0.2 fusion.51
  46.9 0.1 all_to_all.20
  47.0 0.1 copy.22
  47.1 13.4 %all_to_all.31 = f32[32,6,6]{1,2,0:T(8,128)S(1)} all-to-all(f32[32,6,6]{1,2,0:T(8,128)S(1)} %copy.22), channel_id=1, replica_groups=mesh['micro'=8,'macro'=32] {'macro'}, dimensions={0} | all-to-all | bytes 9216 | tf_op jit(solution)/shard_map/all_to_all | solution.py:95
  60.5 0.1 sub.96
  60.6 47.4 %all-gather.4.cloned.1.call-done = bf16[192,6,1024]{2,0,1:T(8,128)(2,1)} async-done(((bf16[192,6,128]{2,0,1:T(8,128)(2,1)}), bf16[192,6,1024]{2,0,1:T(8,128)(2,1)}) %all-gather.4.cloned.1.call-update) | async-done | bytes 2359312 | tf_op jit(solution)/shard_map/all_gather | solution.py:105
  108.0 6.5 %fusion.34 = f32[192,6,128]{2,0,1:T(8,128)S(1)} fusion(bf16[1,6,128,6,1024]{4,2,3,1,0:T(8,128)(2,1)} %param.7, bf16[192,6,1024]{2,0,1:T(8,128)(2,1)} %all-gather.4.cloned.1.call-done, f32[192,6]{0,1:T(8,128)S(1)} %sub.96), kind=kOutput, calls=%fused_computation.14 | convolution fusion | flops 1812086784 | bytes 12390912 | tf_op jit(solution)/shard_map/dot_general | solution.py:106
  114.6 0.1 multiply_add_fusion.1
  114.7 0.1 multiply_multiply_fusion.2
  114.8 0.1 maximum_multiply_fusion.1
  114.9 0.8 fusion.43
  115.7 0.0 all-gather.6.cloned.1.call-update
  115.7 0.0 all-gather.8.cloned.1.call-start
  115.7 64.1 %all-gather.6.cloned.1.call-done = bf16[192,6,1024]{2,0,1:T(8,128)(2,1)} async-done(((bf16[192,6,128]{2,0,1:T(8,128)(2,1)}), bf16[192,6,1024]{2,0,1:T(8,128)(2,1)}) %all-gather.6.cloned.1.call-update) | async-done | bytes 2359312 | tf_op jit(solution)/shard_map/all_gather | solution.py:105
  179.8 6.5 %fusion.29 = f32[192,6,128]{2,0,1:T(8,128)S(1)} fusion(bf16[1,6,128,6,1024]{4,2,3,1,0:T(8,128)(2,1)} %param.7, bf16[192,6,1024]{2,0,1:T(8,128)(2,1)} %all-gather.6.cloned.1.call-done, f32[192,6]{0,1:T(8,128)S(1)} %sub.96), kind=kOutput, calls=%fused_computation.13 | convolution fusion | flops 1812086784 | bytes 12390912 | tf_op jit(solution)/shard_map/dot_general | solution.py:106
  186.4 0.1 multiply_add_fusion
  186.5 0.1 multiply_multiply_fusion.1
  186.6 0.1 maximum_multiply_fusion.2
  186.7 0.8 fusion.44
  187.5 0.0 all-gather.8.cloned.1.call-update
  187.5 0.6 reduce_sum.109
  188.1 63.5 %all-gather.8.cloned.1.call-done = bf16[192,6,1024]{2,0,1:T(8,128)(2,1)} async-done(((bf16[192,6,128]{2,0,1:T(8,128)(2,1)}), bf16[192,6,1024]{2,0,1:T(8,128)(2,1)}) %all-gather.8.cloned.1.call-update) | async-done | bytes 2359312 | tf_op jit(solution)/shard_map/all_gather | solution.py:105
  251.6 6.5 %fusion.24 = f32[192,6,128]{2,0,1:T(8,128)S(1)} fusion(bf16[1,6,128,6,1024]{4,2,3,1,0:T(8,128)(2,1)} %param.7, bf16[192,6,1024]{2,0,1:T(8,128)(2,1)} %all-gather.8.cloned.1.call-done, f32[192,6]{0,1:T(8,128)S(1)} %sub.96), kind=kOutput, calls=%fused_computation.12 | convolution fusion | flops 1812086784 | bytes 12390912 | tf_op jit(solution)/shard_map/dot_general | solution.py:106
  258.2 0.1 multiply_reduce_fusion
  258.4 0.3 fusion.45
  258.7 18.7 %all-reduce.2 = (f32[192,6]{0,1:T(8,128)S(1)}, f32[]{:T(128)}) all-reduce(f32[192,6]{0,1:T(8,128)S(1)} %fusion.45, f32[]{:T(128)} %reduce_sum.109), channel_id=1, replica_groups=mesh['micro'=8,'macro'=32] {'micro'}, use_global_device_ids=true, to_apply=%region_11.12 | all-reduce | flops 1153 | bytes 9224 | tf_op jit(solution)/shard_map/psum | solution.py:118
  277.5 0.6 broadcast_divide_fusion
  278.1 0.1 all_to_all.24
  278.2 0.7 copy.34
  279.0 13.4 %all-to-all-start.3 = ((f32[32,6,6]{1,2,0:T(8,128)}), f32[32,6,6]{1,2,0:T(8,128)S(1)}, u32[]{:S(2)}, u32[]{:S(2)}) async-start(f32[32,6,6]{1,2,0:T(8,128)} %copy.34), calls=%async_computation.3 | async-start | bytes 262144 | tf_op jit(solution)/shard_map/all_to_all | solution.py:122
  292.3 1.2 copy.32
  293.6 8.0 %all-to-all-done.3 = f32[32,6,6]{1,2,0:T(8,128)S(1)} async-done(((f32[32,6,6]{1,2,0:T(8,128)}), f32[32,6,6]{1,2,0:T(8,128)S(1)}, u32[]{:S(2)}, u32[]{:S(2)}) %all-to-all-start.3) | async-done | bytes 4640 | tf_op jit(solution)/shard_map/all_to_all | solution.py:122
  301.6 4.1 %all-to-all-start.2 = ((f32[192,6,128]{2,1,0:T(8,128)}), f32[192,6,128]{2,1,0:T(8,128)S(1)}, u32[]{:S(2)}, u32[]{:S(2)}) async-start(f32[192,6,128]{2,1,0:T(8,128)} %copy.32), calls=%async_computation.2 | async-start | bytes 1572864 | tf_op jit(solution)/shard_map/all_to_all | solution.py:121
  305.8 0.1 all_to_all.26
  305.9 0.2 fusion.49
  306.1 0.1 reshape.386
  306.2 0.1 slice.194
  306.3 2.3 collective-permute-start
  308.5 3.3 collective-permute-start.1
  311.8 0.1 fusion.60
  311.9 0.7 collective-permute-done.1
  312.7 0.1 stack.12
  312.8 0.1 stack.13
  312.8 0.1 stack.14
  312.9 0.6 pad_maximum_fusion
  313.5 15.1 %all-to-all-done.2 = f32[192,6,128]{2,1,0:T(8,128)S(1)} async-done(((f32[192,6,128]{2,1,0:T(8,128)}), f32[192,6,128]{2,1,0:T(8,128)S(1)}, u32[]{:S(2)}, u32[]{:S(2)}) %all-to-all-start.2) | async-done | bytes 589856 | tf_op jit(solution)/shard_map/all_to_all | solution.py:121
  328.6 1.1 fusion.39
  (35 shorter events, 0.6 us)
Async XLA Ops:
  7.2 2.4 copy-start
  7.2 15.4 %copy-start.5 = (s32[1,128]{1,0:T(1,128)S(1)}, s32[1,128]{1,0:T(1,128)}, u32[]{:S(2)}) copy-start(s32[1,128]{1,0:T(1,128)} %param.10) | copy-start | bytes 1540
  7.2 15.4 %copy-start.2 = (f32[1,3,128]{2,0,1:T(1,128)S(1)}, f32[1,3,128]{2,0,1:T(1,128)}, u32[]{:S(2)}) copy-start(f32[1,3,128]{2,0,1:T(1,128)} %param.8) | copy-start | bytes 4612
  11.3 33.8 %all-to-all-start.1 = ((f32[192,6,128]{2,1,0:T(8,128)}), f32[192,6,128]{2,1,0:T(8,128)S(1)}, u32[]{:S(2)}, u32[]{:S(2)}) async-start(f32[192,6,128]{2,1,0:T(8,128)} %copy.26), calls=%async_computation.1 | async-start | bytes 1572864 | tf_op jit(solution)/shard_map/all_to_all | solution.py:94
  22.5 85.5 %all-gather.4.cloned.1.call-start = ((), (), s32[]{:S(2)}) async-start(), calls=%async_computation.4 | async-start | bytes 2654208 | tf_op jit(solution)/shard_map/all_gather | solution.py:105
  45.7 1.0 copy-start.4
  46.6 133.2 %all-gather.6.cloned.1.call-start = ((), (), s32[]{:S(2)}) async-start(), calls=%async_computation.5 | async-start | bytes 2654208 | tf_op jit(solution)/shard_map/all_gather | solution.py:105
  115.7 135.9 %all-gather.8.cloned.1.call-start = ((), (), s32[]{:S(2)}) async-start(), calls=%async_computation.6 | async-start | bytes 2654208 | tf_op jit(solution)/shard_map/all_gather | solution.py:105
  186.5 1.0 copy-start.3
  279.0 22.6 %all-to-all-start.3 = ((f32[32,6,6]{1,2,0:T(8,128)}), f32[32,6,6]{1,2,0:T(8,128)S(1)}, u32[]{:S(2)}, u32[]{:S(2)}) async-start(f32[32,6,6]{1,2,0:T(8,128)} %copy.34), calls=%async_computation.3 | async-start | bytes 262144 | tf_op jit(solution)/shard_map/all_to_all | solution.py:122
  301.6 27.0 %all-to-all-start.2 = ((f32[192,6,128]{2,1,0:T(8,128)}), f32[192,6,128]{2,1,0:T(8,128)S(1)}, u32[]{:S(2)}, u32[]{:S(2)}) async-start(f32[192,6,128]{2,1,0:T(8,128)} %copy.32), calls=%async_computation.2 | async-start | bytes 1572864 | tf_op jit(solution)/shard_map/all_to_all | solution.py:121
  306.1 23.6 %copy-start.1 = (f32[6,64]{1,0:T(8,128)}, f32[6,64]{1,0:T(8,128)S(1)}, u32[]{:S(2)}) copy-start(f32[6,64]{1,0:T(8,128)S(1)} %fusion.49) | copy-start | bytes 4612
  306.3 5.7 %collective-permute-start = (f32[3,1,8,8]{3,2,1,0:T(8,128)S(1)}, f32[3,1,8,8]{3,2,1,0:T(8,128)S(1)}, u32[]{:S(2)}, u32[]{:S(2)}) collective-permute-start(f32[3,1,8,8]{3,2,1,0:T(8,128)S(1)} %bitcast.154), channel_id=1, source_target_pairs={{1,0},{2,1},{3,2},{4,3},{5,4},{6,5},{7,6},{8,7},{9,8},{10,9},{11,1... | collective-permute-start | bytes 2312 | tf_op jit(solution)/shard_map/ppermute | solution.py:25
  308.5 4.1 %collective-permute-start.1 = (f32[3,1,8,8]{3,2,1,0:T(8,128)S(1)}, f32[3,1,8,8]{3,2,1,0:T(8,128)S(1)}, u32[]{:S(2)}, u32[]{:S(2)}) collective-permute-start(f32[3,1,8,8]{3,2,1,0:T(8,128)S(1)} %bitcast.155), channel_id=1, source_target_pairs={{0,1},{1,2},{2,3},{3,4},{4,5},{5,6},{6,7},{7,8},{8,9},{9,10},{10,1... | collective-permute-start | bytes 2312 | tf_op jit(solution)/shard_map/ppermute | solution.py:23
Sparse Core Ops, SparseCore 0:
  46.8 61.2 all-gather.3
  115.8 63.9 all-gather.5
  187.6 63.9 all-gather.7
where the time goes:
time: 337 us; the launch traced here: 336 us
  waiting for transfers between devices  221 us (66%)
  starting transfers between devices  34.3 us (10%)
  blocking collectives  32.1 us (10%)
  matrix products  21.5 us (6%)
  between operations  14.2 us (4%)
  other arithmetic  8.06 us (2%)
  local copies, waits for them, and re-layouts  4.58 us (1%)
    all_gather x3, waiting for transfers between devices, local(): gathered = lax.all_gather(polar_low, 'micro', axis=2, tiled=True)  175 us
    all_to_all x1, waiting for transfers between devices, local(): lax.all_to_all(bucket_state, 'macro', split_axis=0, concat_axis=0, tiled=...  22.5 us
    dot_general x3, matrix products, local(): lax.dot_general(gathered, coupling, contract, preferred_element_type=jnp....  19.6 us
    psum x1, blocking collectives, local(): summed, total_weight = lax.psum((weighted, weight_total), 'micro')  18.7 us
    all_to_all x1, waiting for transfers between devices, local(): lax.all_to_all(strain, 'macro', split_axis=0, concat_axis=0, tiled=True)  15.1 us
    all_to_all x1, starting transfers between devices, local(): lax.all_to_all(averaged, 'macro', split_axis=0, concat_axis=0, tiled=True)  13.4 us
    all_to_all x1, blocking collectives, local(): lax.all_to_all(bucket_target, 'macro', split_axis=0, concat_axis=0, tiled...  13.4 us
    all_to_all x1, starting transfers between devices, local(): lax.all_to_all(bucket_state, 'macro', split_axis=0, concat_axis=0, tiled=...  11.1 us
  transfers between devices with their start and end apart: 8, of which 7 were waited for; matrix products, arithmetic and copies ran while one was open for 1% of the time, Pallas kernels for 0%

commit v1 on v0

v1 whole, which is shorter than its diff:
```python
import functools

import jax
import jax.numpy as jnp
from jax import lax
from jax.experimental import pallas as pl
from jax.experimental.pallas import tpu as pltpu
from jax.sharding import PartitionSpec as P

MESH = pl.DeviceIdType.MESH
HIGHEST = lax.Precision.HIGHEST
ITERS = 3
CHUNKS = 3
HOMES = 32
ROWS = 64
STAGES = ITERS * CHUNKS
MSG = 16


def law(strain, lam, mu, hard, flag):
    tr = strain[0] + strain[1] + strain[2]
    third = tr / 3.0
    dev = [strain[0] - third, strain[1] - third, strain[2] - third, strain[3], strain[4], strain[5]]
    square = (dev[0] * dev[0] + dev[1] * dev[1] + dev[2] * dev[2]) + 2.0 * (
        dev[3] * dev[3] + dev[4] * dev[4] + dev[5] * dev[5]
    )
    soft = lax.rsqrt(1.0 + hard * square)
    scale = 2.0 * (mu * (1.0 + flag * (soft - 1.0)))
    bulk = (lam + 2.0 * mu / 3.0) * tr
    return [scale * dev[a] + bulk if a < 3 else scale * dev[a] for a in range(6)], tr


def kernel(
    w_hbm, moduli_ref, fraction_ref, plastic_ref, id_ref, strain_ref, state_ref,
    home_ref, hom_ref, res_ref,
    w, g, tx, rx, ty, ry, tg, ebuf, pacc, px, rt, rr, st, sn,
    w_sem, in_send, in_recv, ag_send, ag_recv, out_send, out_recv, p_send, p_recv, r_send, r_recv, s_send, s_recv,
):
    micro, me = lax.axis_index("micro"), lax.axis_index("macro")
    x, r = micro // 2, micro % 2
    xl, xr, xo = lax.rem(x + 3, 4), lax.rem(x + 1, 4), lax.rem(x + 2, 4)
    left, right, across = xl * 2 + r, xr * 2 + r, x * 2 + (1 - r)
    across_left, across_right = xl * 2 + (1 - r), xr * 2 + (1 - r)

    load_w = pltpu.make_async_copy(w_hbm, w, w_sem)
    load_w.start()

    barrier = pltpu.get_barrier_semaphore()

    def greet_macro(d, carry):
        pl.semaphore_signal(barrier, inc=1, device_id=(micro, lax.rem(me + d, HOMES)), device_id_type=MESH)
        return carry

    def greet_micro(d, carry):
        pl.semaphore_signal(barrier, inc=1, device_id=(lax.rem(micro + d, 8), me), device_id_type=MESH)
        return carry

    lax.fori_loop(1, HOMES, greet_macro, 0)
    lax.fori_loop(1, 8, greet_micro, 0)

    ids = id_ref[...]
    down = lax.broadcasted_iota(jnp.int32, (64, 64), 0)
    along = lax.broadcasted_iota(jnp.int32, (64, 64), 1)
    id_row = jnp.broadcast_to(ids, (64, 64))
    id_col = jnp.broadcast_to(jnp.sum(jnp.where(down == along, id_row, 0), axis=1, keepdims=True), (64, 64))
    same = id_row == id_col
    slot_row = jnp.sum(jnp.where(same & (down < along), 1, 0), axis=0, keepdims=True) * HOMES + ids
    slot_col = jnp.sum(jnp.where(same & (along < down), 1, 0), axis=1, keepdims=True) * HOMES + jnp.sum(
        jnp.where(down == along, id_row, 0), axis=1, keepdims=True
    )
    slot_col = jnp.broadcast_to(slot_col, (64, 64))
    slot_row = jnp.broadcast_to(slot_row, (64, 64))
    st[...] = jnp.concatenate([slot_row[0:8], jnp.full((8, 64), -1, jnp.int32)], axis=1)

    strain_cols = jnp.concatenate([strain_ref[...], jnp.zeros((122, 64), jnp.float32)], axis=0)
    for c in range(CHUNKS):
        pick = jnp.where(down + c * 64 == slot_row, 1.0, 0.0)
        for b in range(6):
            rows = jnp.dot(pick, state_ref[b], precision=HIGHEST, preferred_element_type=jnp.float32)
            for q in range(2):
                tx[c, pl.ds(b * 2 + q, HOMES, stride=MSG), :] = rows[q * 32 : (q + 1) * 32]
        rows = lax.dot_general(
            pick, strain_cols, (((1,), (1,)), ((), ())), precision=HIGHEST, preferred_element_type=jnp.float32
        )
        for q in range(2):
            tx[c, pl.ds(12 + q, HOMES, stride=MSG), :] = rows[q * 32 : (q + 1) * 32]
            tx[c, pl.ds(14 + q, HOMES, stride=MSG), :] = jnp.zeros((HOMES, 128), jnp.float32)
            ty[c, pl.ds(12 + q, HOMES, stride=MSG), :] = jnp.zeros((HOMES, 128), jnp.float32)
            ty[c, pl.ds(14 + q, HOMES, stride=MSG), :] = jnp.zeros((HOMES, 128), jnp.float32)
    pacc[...] = jnp.zeros((128, 128), jnp.float32)

    pl.semaphore_wait(barrier, 31 + 7)

    def exchange(src, dst, c, send_sem, recv_sem):
        def body(d, carry):
            to = lax.rem(me + d, HOMES)
            pltpu.make_async_remote_copy(
                src_ref=src.at[c, pl.ds(pl.multiple_of(to * MSG, MSG), MSG), :],
                dst_ref=dst.at[c, pl.ds(pl.multiple_of(me * MSG, MSG), MSG), :],
                send_sem=send_sem.at[c],
                recv_sem=recv_sem.at[c],
                device_id=(micro, to),
                device_id_type=MESH,
            ).start()
            return carry

        lax.fori_loop(1, HOMES, body, 0)
        own = pl.ds(pl.multiple_of(me * MSG, MSG), MSG)
        dst[c, own, :] = src[c, own, :]

    def drain(ref, sem):
        pltpu.make_async_copy(ref, ref, sem).wait()

    for c in range(CHUNKS):
        exchange(tx, rx, c, in_send, in_recv)
    for side in range(2):
        pltpu.make_async_remote_copy(
            src_ref=st,
            dst_ref=sn.at[1 - side],
            send_sem=s_send.at[side],
            recv_sem=s_recv.at[1 - side],
            device_id=(micro, lax.rem(me + HOMES - 1 + 2 * side, HOMES)),
            device_id_type=MESH,
        ).start()

    lam, mu, level = moduli_ref[0], moduli_ref[1], moduli_ref[2]
    hard = 4.0 * mu * mu / (level * level)
    flag = plastic_ref[...].astype(jnp.float32)
    fraction = fraction_ref[...]
    total = jnp.sum(fraction, axis=1, keepdims=True)

    def send(s, block, low, high, to, kind):
        pltpu.make_async_remote_copy(
            src_ref=g.at[s, block, low:high],
            dst_ref=g.at[s, block, low:high],
            send_sem=ag_send.at[s],
            recv_sem=ag_recv.at[s, kind],
            device_id=(to, me),
            device_id_type=MESH,
        ).start()

    def polarize(s, strain):
        stress, tr = law(strain, lam, mu, hard, flag)
        for a in range(6):
            tau = stress[a] - (tr + 2.0 * strain[a]) if a < 3 else stress[a] - 2.0 * strain[a]
            g[s, micro, a] = tau.astype(jnp.bfloat16)

    def period(p, carry):
        @pl.when(p < CHUNKS)
        def _():
            drain(rx.at[p, 0 : 31 * MSG], in_recv.at[p])
            strain = [
                jnp.concatenate([rx[p, pl.ds(b * 2 + q, HOMES, stride=MSG), :] for q in range(2)], axis=0)
                for b in range(6)
            ]
            tg[p] = jnp.concatenate([rx[p, pl.ds(12 + q, HOMES, stride=MSG), :] for q in range(2)], axis=0)
            polarize(p, strain)

        @pl.when(p < STAGES)
        def _():
            send(p, micro, 0, 6, right, 0)
            send(p, micro, 0, 6, left, 1)
            send(p, micro, 0, 6, across, 2)

        @pl.when((p >= 1) & (p < STAGES + 1))
        def _():
            s = p - 1
            drain(g.at[s, 0], ag_recv.at[s, 0])
            send(s, left, 0, 3, right, 5)
            send(s, left, 0, 3, across, 3)
            drain(g.at[s, 0], ag_recv.at[s, 1])
            send(s, right, 3, 6, left, 5)
            send(s, right, 3, 6, across, 4)
            drain(g.at[s, 0], ag_recv.at[s, 2])
            send(s, across, 0, 3, left, 5)
            send(s, across, 3, 6, right, 5)

        @pl.when(p >= 2)
        def _():
            s = p - 2
            c = lax.rem(s, CHUNKS)
            drain(g.at[s, 0, 0:3], ag_recv.at[s, 3])
            send(s, across_left, 0, 3, right, 5)
            drain(g.at[s, 0, 0:3], ag_recv.at[s, 4])
            send(s, across_right, 3, 6, left, 5)
            @pl.when(p == 2)
            def _():
                load_w.wait()

            drain(g.at[s, 0:3], ag_recv.at[s, 5])
            columns = [jnp.concatenate([g[s, j, b] for b in range(6)], axis=1) for j in range(8)]
            target = tg[c]
            for a in range(6):
                acc = jnp.zeros((128, ROWS), jnp.float32)
                for j in range(8):
                    rows = jnp.concatenate([w[a, b, :, j * 128 : (j + 1) * 128] for b in range(6)], axis=1)
                    acc = acc + lax.dot_general(
                        rows, columns[j], (((1,), (1,)), ((), ())), preferred_element_type=jnp.float32
                    )
                ebuf[a] = target[:, a : a + 1] - acc.T
            strain = [ebuf[a] for a in range(6)]

            @pl.when(s < STAGES - CHUNKS)
            def _():
                polarize(s + CHUNKS, strain)

            @pl.when(s >= STAGES - CHUNKS)
            def _():
                for b in range(6):
                    for q in range(2):
                        ty[c, pl.ds(b * 2 + q, HOMES, stride=MSG), :] = ebuf[b, q * 32 : (q + 1) * 32]
                exchange(ty, ry, c, out_send, out_recv)
                stress, _ = law(strain, lam, mu, hard, flag)
                lane = lax.broadcasted_iota(jnp.int32, (ROWS, 128), 1)
                sums = pacc[0:ROWS]
                for a in range(6):
                    part = jnp.sum(stress[a] * fraction, axis=1, keepdims=True)
                    sums = jnp.where(lane == c * 8 + a, part, sums)
                pacc[0:ROWS] = sums

        return carry

    lax.fori_loop(0, STAGES + 2, period, 0)

    sums = pacc[...].T[0 : 8 * CHUNKS]
    row = lax.broadcasted_iota(jnp.int32, (8 * CHUNKS, 128), 0)
    px[micro] = jnp.where(row == 6, total, sums)

    def share(d, carry):
        pltpu.make_async_remote_copy(
            src_ref=px.at[micro],
            dst_ref=px.at[micro],
            send_sem=p_send,
            recv_sem=p_recv,
            device_id=(lax.rem(micro + d, 8), me),
            device_id_type=MESH,
        ).start()
        return carry

    lax.fori_loop(1, 8, share, 0)
    drain(px.at[0:7], p_recv)
    sums = px[0]
    for i in range(1, 8):
        sums = sums + px[i]
    mean = sums / sums[6:7]
    mean = jnp.concatenate([mean, jnp.zeros((128 - 8 * CHUNKS, 128), jnp.float32)], axis=0).T
    for d in range(3):
        for q in range(2):
            part = mean[q * 32 : (q + 1) * 32]
            if d != 1:
                part = pltpu.roll(part, 1 if d == 0 else 31, 0)
            rt[pl.ds(d * 2 + q, HOMES, stride=8), :] = part
    for spare in (6, 7):
        rt[pl.ds(spare, HOMES, stride=8), :] = jnp.zeros((HOMES, 128), jnp.float32)

    def give(d, carry):
        to = lax.rem(me + d, HOMES)
        pltpu.make_async_remote_copy(
            src_ref=rt.at[pl.ds(pl.multiple_of(to * 8, 8), 8), :],
            dst_ref=rr.at[pl.ds(pl.multiple_of(me * 8, 8), 8), :],
            send_sem=r_send,
            recv_sem=r_recv,
            device_id=(micro, to),
            device_id_type=MESH,
        ).start()
        return carry

    lax.fori_loop(1, HOMES, give, 0)
    own = pl.ds(pl.multiple_of(me * 8, 8), 8)
    rr[own, :] = rt[own, :]

    for c in range(CHUNKS):
        drain(ry.at[c, 0 : 31 * MSG], out_recv.at[c])
        pick = jnp.where(along + c * 64 == slot_col, 1.0, 0.0)
        for b in range(6):
            rows = jnp.concatenate([ry[c, pl.ds(b * 2 + q, HOMES, stride=MSG), :] for q in range(2)], axis=0)
            part = jnp.dot(pick, rows, precision=HIGHEST, preferred_element_type=jnp.float32)
            home_ref[b] = part if c == 0 else home_ref[b] + part

    for side in range(2):
        drain(sn.at[side], s_recv.at[side])
    drain(rr.at[0 : 31 * 8], r_recv)
    slots = [sn[0][0:1], st[0:1], sn[1][0:1]]
    down2 = lax.broadcasted_iota(jnp.int32, (64, 128), 0)
    hom = []
    for d in range(3):
        rows = jnp.concatenate([rr[pl.ds(d * 2 + q, HOMES, stride=8), :] for q in range(2)], axis=0).T
        slab = jnp.zeros((8, 128), jnp.float32)
        for c in range(CHUNKS):
            pick = jnp.where(down2 + c * 64 == jnp.broadcast_to(slots[d], (64, 128)), 1.0, 0.0)
            slab = slab + jnp.dot(
                rows[c * 8 : (c + 1) * 8], pick, precision=HIGHEST, preferred_element_type=jnp.float32
            )
        hom.append(slab)
    here = hom[1]
    hom_ref[...] = here[0:6, 0:64]
    lane = lax.broadcasted_iota(jnp.int32, (8, 128), 1)
    along_x = 0.5 * (pltpu.roll(here, 120, 1) - pltpu.roll(here, 8, 1))
    above = jnp.where(lane % 8 == 7, 0.0, pltpu.roll(here, 127, 1))
    below = jnp.where(lane % 8 == 0, 0.0, pltpu.roll(here, 1, 1))
    along_y = 0.5 * (above - below)
    along_z = 0.5 * (jnp.where(me == HOMES - 1, 0.0, hom[2]) - jnp.where(me == 0, 0.0, hom[0]))
    res_x = along_x[0:1] + along_y[5:6] + along_z[4:5]
    res_y = along_x[5:6] + along_y[1:2] + along_z[3:4]
    res_z = along_x[4:5] + along_y[3:4] + along_z[2:3]
    res_ref[...] = jnp.concatenate([res_x, res_y, res_z], axis=0)[:, 0:64]

    for c in range(CHUNKS):
        drain(tx.at[c, 0 : 31 * MSG], in_send.at[c])
        drain(ty.at[c, 0 : 31 * MSG], out_send.at[c])
    for side in range(2):
        drain(st, s_send.at[side])

    def sent(s, carry):
        drain(g.at[s, 0:7], ag_send.at[s])
        return carry

    lax.fori_loop(0, STAGES, sent, 0)
    drain(px.at[0:7], p_send)
    drain(rt.at[0 : 31 * 8], r_send)


def local(interaction, cluster_moduli, cluster_fraction, plastic_flag, micro_id, macro_strain, cluster_state):
    vmem = pl.BlockSpec(memory_space=pltpu.VMEM)
    home, hom, res = pl.pallas_call(
        kernel,
        out_shape=(
            jax.ShapeDtypeStruct((6, 64, 128), jnp.float32),
            jax.ShapeDtypeStruct((6, 64), jnp.float32),
            jax.ShapeDtypeStruct((3, 64), jnp.float32),
        ),
        in_specs=[pl.BlockSpec(memory_space=pl.ANY)] + [vmem] * 6,
        out_specs=(vmem, vmem, vmem),
        scratch_shapes=[
            pltpu.VMEM((6, 6, 128, 1024), jnp.bfloat16),
            pltpu.VMEM((STAGES, 8, 6, ROWS, 128), jnp.bfloat16),
            pltpu.VMEM((CHUNKS, HOMES * MSG, 128), jnp.float32),
            pltpu.VMEM((CHUNKS, HOMES * MSG, 128), jnp.float32),
            pltpu.VMEM((CHUNKS, HOMES * MSG, 128), jnp.float32),
            pltpu.VMEM((CHUNKS, HOMES * MSG, 128), jnp.float32),
            pltpu.VMEM((CHUNKS, ROWS, 128), jnp.float32),
            pltpu.VMEM((6, ROWS, 128), jnp.float32),
            pltpu.VMEM((128, 128), jnp.float32),
            pltpu.VMEM((8, 8 * CHUNKS, 128), jnp.float32),
            pltpu.VMEM((HOMES * 8, 128), jnp.float32),
            pltpu.VMEM((HOMES * 8, 128), jnp.float32),
            pltpu.VMEM((8, 128), jnp.int32),
            pltpu.VMEM((2, 8, 128), jnp.int32),
            pltpu.SemaphoreType.DMA,
            pltpu.SemaphoreType.DMA((CHUNKS,)),
            pltpu.SemaphoreType.DMA((CHUNKS,)),
            pltpu.SemaphoreType.DMA((STAGES,)),
            pltpu.SemaphoreType.DMA((STAGES, 6)),
            pltpu.SemaphoreType.DMA((CHUNKS,)),
            pltpu.SemaphoreType.DMA((CHUNKS,)),
            pltpu.SemaphoreType.DMA,
            pltpu.SemaphoreType.DMA,
            pltpu.SemaphoreType.DMA,
            pltpu.SemaphoreType.DMA,
            pltpu.SemaphoreType.DMA((2,)),
            pltpu.SemaphoreType.DMA((2,)),
        ],
        compiler_params=pltpu.CompilerParams(
            collective_id=0, has_side_effects=True, vmem_limit_bytes=48 * 2**20
        ),
    )(
        jnp.transpose(interaction[0], (0, 2, 1, 3)),
        jnp.transpose(cluster_moduli, (1, 0, 2)),
        cluster_fraction,
        plastic_flag,
        micro_id.reshape(1, -1),
        macro_strain.T,
        jnp.transpose(cluster_state, (1, 0, 2)),
    )
    return jnp.transpose(home, (1, 0, 2)), hom, res


def solution(mesh):
    placed = (
        P("macro", None, "micro", None, None),
        P("macro", None, "micro"),
        P("macro", "micro"),
        P("macro", "micro"),
        P("macro", None),
        P("macro", None),
        P("macro", None, "micro"),
    )
    return jax.shard_map(
        local,
        mesh=mesh,
        in_specs=placed,
        out_specs=(P("macro", None, "micro"), P(None, "macro"), P(None, "macro")),
        check_vma=False,
    )
```

time: 337 us -> 134 us (0.40)
  waiting for transfers between devices: 221 us -> 0 us
  Pallas kernels: 0 us -> 127 us
  starting transfers between devices: 34.3 us -> 0 us
  blocking collectives: 32.1 us -> 0 us
  matrix products: 21.5 us -> 0 us
  between operations: 14.2 us -> 0.66 us
  other arithmetic: 8.06 us -> 0 us
    all_gather x3 -> x0, waiting for transfers between devices: 175 us -> none  [local(): gathered = lax.all_gather(polar_low, 'micro', axis=2, tiled=True)]
    pallas_call x0 -> x1, Pallas kernels: none -> 127 us  [local(): pl.pallas_call(kernel, out_shape=(jax.ShapeDtypeStruct((6, 64, 128), jnp....]
    all_to_all x3 -> x0, waiting for transfers between devices: 45.6 us -> none  [the longest x1 22.5 us: local(): lax.all_to_all(bucket_state, 'macro', split_axis=0, concat_axis=0, tiled=...]
    all_to_all x3 -> x0, starting transfers between devices: 28.6 us -> none  [the longest x1 13.4 us: local(): lax.all_to_all(averaged, 'macro', split_axis=0, concat_axis=0, tiled=True)]
    dot_general x7 -> x0, matrix products: 21.5 us -> none  [the longest x3 19.6 us: local(): lax.dot_general(gathered, coupling, contract, preferred_element_type=jnp....]
    psum x1 -> x0, blocking collectives: 18.7 us -> none  [local(): summed, total_weight = lax.psum((weighted, weight_total), 'micro')]
    all_to_all x1 -> x0, blocking collectives: 13.4 us -> none  [local(): lax.all_to_all(bucket_target, 'macro', split_axis=0, concat_axis=0, tiled...]
    unnamed x12 -> x15, local copies, waits for them, and re-layouts: 0.03 us -> 6.1 us
  transfers between devices with their start and end apart: 8 -> 0, of which waited for: 7 -> 0; matrix products, arithmetic and copies ran while one was open for 1% -> 0% of each run, Pallas kernels for 0% -> 0%
where the time goes in v1:
time: 134 us
  Pallas kernels  127 us (95%)
  local copies, waits for them, and re-layouts  6.1 us (5%)
    pallas_call x1, Pallas kernels, local(): pl.pallas_call(kernel, out_shape=(jax.ShapeDtypeStruct((6, 64, 128), jnp....  127 us
    unnamed x15, local copies, waits for them, and re-layouts  6.1 us

profile of v1, /device:TPU:1, one launch (start us, length us, event | category | flops | bytes accessed | tf_op | source)
XLA Modules:
  0.0 133.8 jit_solution(792125212116773629)
XLA Ops:
  0.6 0.0 copy-start
  0.6 0.9 copy-done
  1.6 0.0 copy-start.1
  1.6 0.7 copy-done.1
  2.2 0.0 copy-start.2
  2.2 0.7 copy-done.2
  2.9 0.0 copy-start.3
  2.9 0.7 copy-done.3
  3.6 0.0 copy-start.4
  3.6 0.7 copy-done.4
  4.2 0.0 copy-start.5
  4.2 0.7 copy-done.5
  4.9 127.1 %shard_map.94 = (f32[6,64,128]{2,1,0:T(8,128)S(1)}, f32[6,64]{1,0:T(8,128)S(1)}, f32[3,64]{1,0:T(4,128)S(1)}) custom-call(bf16[6,6,128,1024]{3,2,1,0:T(8,128)(2,1)} %bitcast.13, f32[3,1,128]{2,1,0:T(1,128)S(1)} %bitcast.11, f32[1,128]{1,0:T(1,128)S(1)} %copy-done.3, s32[1,128]{1,0:T(1,128)S(1)} %copy-done.4, s32[1,64]{1,0:T(1,128)S(1)} %bitcast.12, ...), custom_call_target="tpu_custom_call" | custom-call | tf_op jit(solution)/shard_map/pallas_call | solution.py:325
  132.0 0.7 copy.13
  132.7 0.6 copy.14
  133.2 0.6 copy.15
Async XLA Ops:
  0.6 0.9 copy-start
  1.6 0.7 copy-start.1
  2.2 0.7 copy-start.2
  2.9 0.7 copy-start.3
  3.6 0.7 copy-start.4
  4.2 0.7 copy-start.5

commit v2 on v1

--- a/solution.py
+++ b/solution.py
@@ -31,10 +31,10 @@
 
 
 def kernel(
-    w_hbm, moduli_ref, fraction_ref, plastic_ref, id_ref, strain_ref, state_ref,
+    w_hbm, moduli_hbm, fraction_hbm, plastic_hbm, id_hbm, strain_hbm, state_hbm,
     home_ref, hom_ref, res_ref,
-    w, g, tx, rx, ty, ry, tg, ebuf, pacc, px, rt, rr, st, sn,
-    w_sem, in_send, in_recv, ag_send, ag_recv, out_send, out_recv, p_send, p_recv, r_send, r_recv, s_send, s_recv,
+    w, moduli_ref, fraction_ref, plastic_ref, id_ref, strain_ref, state_ref, acc, g, tx, rx, ty, ry, tg, ebuf, pacc, px, rt, rr, st, sn,
+    w_sem, i_sem, in_send, in_recv, ag_send, ag_recv, out_send, out_recv, p_send, p_recv, r_send, r_recv, s_send, s_recv,
 ):
     micro, me = lax.axis_index("micro"), lax.axis_index("macro")
     x, r = micro // 2, micro % 2
@@ -42,22 +42,39 @@
     left, right, across = xl * 2 + r, xr * 2 + r, x * 2 + (1 - r)
     across_left, across_right = xl * 2 + (1 - r), xr * 2 + (1 - r)
 
+    loads = [
+        pltpu.make_async_copy(src, dst, i_sem.at[i])
+        for i, (src, dst) in enumerate(
+            [
+                (id_hbm, id_ref), (state_hbm, state_ref), (strain_hbm, strain_ref),
+                (moduli_hbm, moduli_ref), (fraction_hbm, fraction_ref), (plastic_hbm, plastic_ref),
+            ]
+        )
+    ]
+    for load in loads:
+        load.start()
     load_w = pltpu.make_async_copy(w_hbm, w, w_sem)
     load_w.start()
 
     barrier = pltpu.get_barrier_semaphore()
 
-    def greet_macro(d, carry):
-        pl.semaphore_signal(barrier, inc=1, device_id=(micro, lax.rem(me + d, HOMES)), device_id_type=MESH)
+    def far(i):
+        half = (i + 1) // 2
+        return lax.rem(me + HOMES + 16 + half * (1 - 2 * (i % 2)), HOMES)
+
+    def greet_macro(i, carry):
+        pl.semaphore_signal(barrier, inc=1, device_id=(micro, far(i)), device_id_type=MESH)
         return carry
 
     def greet_micro(d, carry):
         pl.semaphore_signal(barrier, inc=1, device_id=(lax.rem(micro + d, 8), me), device_id_type=MESH)
         return carry
 
-    lax.fori_loop(1, HOMES, greet_macro, 0)
+    lax.fori_loop(0, HOMES - 1, greet_macro, 0)
     lax.fori_loop(1, 8, greet_micro, 0)
 
+    for load in loads:
+        load.wait()
     ids = id_ref[...]
     down = lax.broadcasted_iota(jnp.int32, (64, 64), 0)
     along = lax.broadcasted_iota(jnp.int32, (64, 64), 1)
@@ -92,8 +109,8 @@
     pl.semaphore_wait(barrier, 31 + 7)
 
     def exchange(src, dst, c, send_sem, recv_sem):
-        def body(d, carry):
-            to = lax.rem(me + d, HOMES)
+        def body(i, carry):
+            to = far(i)
             pltpu.make_async_remote_copy(
                 src_ref=src.at[c, pl.ds(pl.multiple_of(to * MSG, MSG), MSG), :],
                 dst_ref=dst.at[c, pl.ds(pl.multiple_of(me * MSG, MSG), MSG), :],
@@ -104,7 +121,7 @@
             ).start()
             return carry
 
-        lax.fori_loop(1, HOMES, body, 0)
+        lax.fori_loop(0, HOMES - 1, body, 0)
         own = pl.ds(pl.multiple_of(me * MSG, MSG), MSG)
         dst[c, own, :] = src[c, own, :]
 
@@ -145,7 +162,28 @@
             tau = stress[a] - (tr + 2.0 * strain[a]) if a < 3 else stress[a] - 2.0 * strain[a]
             g[s, micro, a] = tau.astype(jnp.bfloat16)
 
+    def share(d, carry):
+        pltpu.make_async_remote_copy(
+            src_ref=px.at[micro],
+            dst_ref=px.at[micro],
+            send_sem=p_send,
+            recv_sem=p_recv,
+            device_id=(lax.rem(micro + d, 8), me),
+            device_id_type=MESH,
+        ).start()
+        return carry
+
     def period(p, carry):
+        def partial(s, a, blocks):
+            total_a = None
+            for j in blocks:
+                lanes = pl.ds(pl.multiple_of(j * 128, 128), 128)
+                rows = jnp.concatenate([w[a, b, :, lanes] for b in range(6)], axis=1)
+                columns = jnp.concatenate([g[s, j, b] for b in range(6)], axis=1)
+                part = lax.dot_general(rows, columns, (((1,), (1,)), ((), ())), preferred_element_type=jnp.float32)
+                total_a = part if total_a is None else total_a + part
+            return total_a
+
         @pl.when(p < CHUNKS)
         def _():
             drain(rx.at[p, 0 : 31 * MSG], in_recv.at[p])
@@ -156,11 +194,33 @@
             tg[p] = jnp.concatenate([rx[p, pl.ds(12 + q, HOMES, stride=MSG), :] for q in range(2)], axis=0)
             polarize(p, strain)
 
+        @pl.when(p >= 2)
+        def _():
+            s = p - 2
+            drain(g.at[s, 0, 0:3], ag_recv.at[s, 3])
+            drain(g.at[s, 0, 0:3], ag_recv.at[s, 4])
+
+            @pl.when(s < STAGES - 1)
+            def _():
+                send(s, across_left, 0, 3, right, 5)
+                send(s, across_right, 3, 6, left, 5)
+
         @pl.when(p < STAGES)
         def _():
             send(p, micro, 0, 6, right, 0)
             send(p, micro, 0, 6, left, 1)
             send(p, micro, 0, 6, across, 2)
+
+        @pl.when(p >= 2)
+        def _():
+            s = p - 2
+
+            @pl.when(p == 2)
+            def _():
+                load_w.wait()
+
+            for a in range(6):
+                acc[a] = partial(s, a, [micro, left, right, across])
 
         @pl.when((p >= 1) & (p < STAGES + 1))
         def _():
@@ -175,29 +235,20 @@
             send(s, across, 0, 3, left, 5)
             send(s, across, 3, 6, right, 5)
 
+            @pl.when(s == STAGES - 1)
+            def _():
+                send(s, across, 0, 6, xo * 2 + r, 5)
+
+
         @pl.when(p >= 2)
         def _():
             s = p - 2
             c = lax.rem(s, CHUNKS)
-            drain(g.at[s, 0, 0:3], ag_recv.at[s, 3])
-            send(s, across_left, 0, 3, right, 5)
-            drain(g.at[s, 0, 0:3], ag_recv.at[s, 4])
-            send(s, across_right, 3, 6, left, 5)
-            @pl.when(p == 2)
-            def _():
-                load_w.wait()
-
             drain(g.at[s, 0:3], ag_recv.at[s, 5])
-            columns = [jnp.concatenate([g[s, j, b] for b in range(6)], axis=1) for j in range(8)]
             target = tg[c]
             for a in range(6):
-                acc = jnp.zeros((128, ROWS), jnp.float32)
-                for j in range(8):
-                    rows = jnp.concatenate([w[a, b, :, j * 128 : (j + 1) * 128] for b in range(6)], axis=1)
-                    acc = acc + lax.dot_general(
-                        rows, columns[j], (((1,), (1,)), ((), ())), preferred_element_type=jnp.float32
-                    )
-                ebuf[a] = target[:, a : a + 1] - acc.T
+                rest = partial(s, a, [xo * 2 + r, across_left, across_right, xo * 2 + (1 - r)])
+                ebuf[a] = target[:, a : a + 1] - (acc[a] + rest).T
             strain = [ebuf[a] for a in range(6)]
 
             @pl.when(s < STAGES - CHUNKS)
@@ -206,10 +257,6 @@
 
             @pl.when(s >= STAGES - CHUNKS)
             def _():
-                for b in range(6):
-                    for q in range(2):
-                        ty[c, pl.ds(b * 2 + q, HOMES, stride=MSG), :] = ebuf[b, q * 32 : (q + 1) * 32]
-                exchange(ty, ry, c, out_send, out_recv)
                 stress, _ = law(strain, lam, mu, hard, flag)
                 lane = lax.broadcasted_iota(jnp.int32, (ROWS, 128), 1)
                 sums = pacc[0:ROWS]
@@ -218,26 +265,22 @@
                     sums = jnp.where(lane == c * 8 + a, part, sums)
                 pacc[0:ROWS] = sums
 
+                @pl.when(s == STAGES - 1)
+                def _():
+                    rows = pacc[...].T[0 : 8 * CHUNKS]
+                    row = lax.broadcasted_iota(jnp.int32, (8 * CHUNKS, 128), 0)
+                    px[micro] = jnp.where(row == 6, total, rows)
+                    lax.fori_loop(1, 8, share, 0)
+
+                for b in range(6):
+                    for q in range(2):
+                        ty[c, pl.ds(b * 2 + q, HOMES, stride=MSG), :] = ebuf[b, q * 32 : (q + 1) * 32]
+                exchange(ty, ry, c, out_send, out_recv)
+
         return carry
 
     lax.fori_loop(0, STAGES + 2, period, 0)
 
-    sums = pacc[...].T[0 : 8 * CHUNKS]
-    row = lax.broadcasted_iota(jnp.int32, (8 * CHUNKS, 128), 0)
-    px[micro] = jnp.where(row == 6, total, sums)
-
-    def share(d, carry):
-        pltpu.make_async_remote_copy(
-            src_ref=px.at[micro],
-            dst_ref=px.at[micro],
-            send_sem=p_send,
-            recv_sem=p_recv,
-            device_id=(lax.rem(micro + d, 8), me),
-            device_id_type=MESH,
-        ).start()
-        return carry
-
-    lax.fori_loop(1, 8, share, 0)
     drain(px.at[0:7], p_recv)
     sums = px[0]
     for i in range(1, 8):
@@ -253,8 +296,8 @@
     for spare in (6, 7):
         rt[pl.ds(spare, HOMES, stride=8), :] = jnp.zeros((HOMES, 128), jnp.float32)
 
-    def give(d, carry):
-        to = lax.rem(me + d, HOMES)
+    def give(i, carry):
+        to = far(i)
         pltpu.make_async_remote_copy(
             src_ref=rt.at[pl.ds(pl.multiple_of(to * 8, 8), 8), :],
             dst_ref=rr.at[pl.ds(pl.multiple_of(me * 8, 8), 8), :],
@@ -265,7 +308,7 @@
         ).start()
         return carry
 
-    lax.fori_loop(1, HOMES, give, 0)
+    lax.fori_loop(0, HOMES - 1, give, 0)
     own = pl.ds(pl.multiple_of(me * 8, 8), 8)
     rr[own, :] = rt[own, :]
 
@@ -329,10 +372,17 @@
             jax.ShapeDtypeStruct((6, 64), jnp.float32),
             jax.ShapeDtypeStruct((3, 64), jnp.float32),
         ),
-        in_specs=[pl.BlockSpec(memory_space=pl.ANY)] + [vmem] * 6,
+        in_specs=[pl.BlockSpec(memory_space=pltpu.HBM)] * 7,
         out_specs=(vmem, vmem, vmem),
         scratch_shapes=[
             pltpu.VMEM((6, 6, 128, 1024), jnp.bfloat16),
+            pltpu.VMEM((3, 1, 128), jnp.float32),
+            pltpu.VMEM((1, 128), jnp.float32),
+            pltpu.VMEM((1, 128), jnp.int32),
+            pltpu.VMEM((1, 64), jnp.int32),
+            pltpu.VMEM((6, 64), jnp.float32),
+            pltpu.VMEM((6, 64, 128), jnp.float32),
+            pltpu.VMEM((6, 128, ROWS), jnp.float32),
             pltpu.VMEM((STAGES, 8, 6, ROWS, 128), jnp.bfloat16),
             pltpu.VMEM((CHUNKS, HOMES * MSG, 128), jnp.float32),
             pltpu.VMEM((CHUNKS, HOMES * MSG, 128), jnp.float32),
@@ -347,6 +397,7 @@
             pltpu.VMEM((8, 128), jnp.int32),
             pltpu.VMEM((2, 8, 128), jnp.int32),
             pltpu.SemaphoreType.DMA,
+            pltpu.SemaphoreType.DMA((6,)),
             pltpu.SemaphoreType.DMA((CHUNKS,)),
             pltpu.SemaphoreType.DMA((CHUNKS,)),
             pltpu.SemaphoreType.DMA((STAGES,)),
@@ -361,7 +412,7 @@
             pltpu.SemaphoreType.DMA((2,)),
         ],
         compiler_params=pltpu.CompilerParams(
-            collective_id=0, has_side_effects=True, vmem_limit_bytes=48 * 2**20
+            collective_id=0, has_side_effects=True, vmem_limit_bytes=40 * 2**20
         ),
     )(
         jnp.transpose(interaction[0], (0, 2, 1, 3)),

time: 134 us -> 114 us (0.85)
  Pallas kernels: 127 us -> 104 us
  local copies, waits for them, and re-layouts: 6.1 us -> 9.78 us
    pallas_call x1, Pallas kernels: 127 us -> 104 us  [local(): pl.pallas_call(kernel, out_shape=(jax.ShapeDtypeStruct((6, 64, 128), jnp....]
    unnamed x15 -> x17, local copies, waits for them, and re-layouts: 6.1 us -> 9.78 us
where the time goes in v2:
time: 114 us
  Pallas kernels  104 us (91%)
  local copies, waits for them, and re-layouts  9.78 us (9%)
    pallas_call x1, Pallas kernels, local(): pl.pallas_call(kernel, out_shape=(jax.ShapeDtypeStruct((6, 64, 128), jnp....  104 us
    unnamed x17, local copies, waits for them, and re-layouts  9.78 us

profile of v2, /device:TPU:1, one launch (start us, length us, event | category | flops | bytes accessed | tf_op | source)
XLA Modules:
  0.0 114.0 jit_solution(6441874238944313882)
XLA Ops:
  0.6 0.0 copy-start
  0.6 3.7 %copy-done = bf16[1,6,128,6,1024]{4,2,3,1,0:T(8,128)(2,1)S(1)} copy-done((bf16[1,6,128,6,1024]{4,2,3,1,0:T(8,128)(2,1)S(1)}, bf16[1,6,128,6,1024]{4,2,3,1,0:T(8,128)(2,1)}, u32[]{:S(2)}) %copy-start) | copy-done | bytes 9437208
  4.3 0.0 copy-start.1
  4.3 0.9 copy-done.1
  5.2 0.0 copy-start.2
  5.2 0.7 copy-done.2
  5.9 0.0 copy-start.3
  5.9 0.7 copy-done.3
  6.6 0.0 copy-start.4
  6.6 0.7 copy-done.4
  7.3 0.0 copy-start.5
  7.3 0.7 copy-done.5
  7.9 0.0 copy-start.6
  7.9 0.7 copy-done.6
  8.6 103.6 %shard_map.94 = (f32[6,64,128]{2,1,0:T(8,128)S(1)}, f32[6,64]{1,0:T(8,128)S(1)}, f32[3,64]{1,0:T(4,128)S(1)}) custom-call(bf16[6,6,128,1024]{3,2,1,0:T(8,128)(2,1)S(1)} %bitcast.8, f32[3,1,128]{2,1,0:T(1,128)S(1)} %bitcast.12, f32[1,128]{1,0:T(1,128)S(1)} %copy-done.4, s32[1,128]{1,0:T(1,128)S(1)} %copy-done.5, s32[1,64]{1,0:T(1,128)S(1)} %bitcast.13, ...), custom_call_target="tpu_custom_call" | custom-call | tf_op jit(solution)/shard_map/pallas_call | solution.py:368
  112.2 0.7 copy.13
  112.9 0.6 copy.14
  113.4 0.6 copy.15
Async XLA Ops:
  0.6 3.7 %copy-start = (bf16[1,6,128,6,1024]{4,2,3,1,0:T(8,128)(2,1)S(1)}, bf16[1,6,128,6,1024]{4,2,3,1,0:T(8,128)(2,1)}, u32[]{:S(2)}) copy-start(bf16[1,6,128,6,1024]{4,2,3,1,0:T(8,128)(2,1)} %param.7) | copy-start | bytes 28311556
  4.3 0.9 copy-start.1
  5.2 0.7 copy-start.2
  5.9 0.7 copy-start.3
  6.6 0.7 copy-start.4
  7.3 0.7 copy-start.5
  7.9 0.7 copy-start.6

commit v3 on v2

--- a/solution.py
+++ b/solution.py
@@ -368,11 +368,11 @@
     home, hom, res = pl.pallas_call(
         kernel,
         out_shape=(
-            jax.ShapeDtypeStruct((6, 64, 128), jnp.float32),
-            jax.ShapeDtypeStruct((6, 64), jnp.float32),
-            jax.ShapeDtypeStruct((3, 64), jnp.float32),
+            pltpu.VMEM((6, 64, 128), jnp.float32),
+            pltpu.VMEM((6, 64), jnp.float32),
+            pltpu.VMEM((3, 64), jnp.float32),
         ),
-        in_specs=[pl.BlockSpec(memory_space=pltpu.HBM)] * 7,
+        in_specs=[pl.BlockSpec(memory_space=pl.ANY)] * 7,
         out_specs=(vmem, vmem, vmem),
         scratch_shapes=[
             pltpu.VMEM((6, 6, 128, 1024), jnp.bfloat16),
@@ -412,7 +412,7 @@
             pltpu.SemaphoreType.DMA((2,)),
         ],
         compiler_params=pltpu.CompilerParams(
-            collective_id=0, has_side_effects=True, vmem_limit_bytes=40 * 2**20
+            collective_id=0, has_side_effects=True, vmem_limit_bytes=56 * 2**20
         ),
     )(
         jnp.transpose(interaction[0], (0, 2, 1, 3)),

time: 114 us -> 105 us (0.921)
  local copies, waits for them, and re-layouts: 9.78 us -> 1.85 us
    unnamed x17 -> x3, local copies, waits for them, and re-layouts: 9.78 us -> 1.85 us
where the time goes in v3:
time: 105 us
  Pallas kernels  103 us (98%)
  local copies, waits for them, and re-layouts  1.85 us (2%)
    pallas_call x1, Pallas kernels, local(): pl.pallas_call(kernel, out_shape=(pltpu.VMEM((6, 64, 128), jnp.float32),...  103 us

profile of v3, /device:TPU:1, one launch (start us, length us, event | category | flops | bytes accessed | tf_op | source)
XLA Modules:
  0.0 105.4 jit_solution(4727055222755591253)
XLA Ops:
  0.6 102.9 %shard_map.94 = (f32[6,64,128]{2,1,0:T(8,128)S(1)}, f32[6,64]{1,0:T(8,128)S(1)}, f32[3,64]{1,0:T(4,128)S(1)}) custom-call(bf16[6,6,128,1024]{3,2,1,0:T(8,128)(2,1)} %bitcast.9, f32[3,1,128]{2,1,0:T(1,128)} %bitcast.12, f32[1,128]{1,0:T(1,128)} %fraction_hbm.1, s32[1,128]{1,0:T(1,128)} %plastic_hbm.1, s32[1,64]{1,0:T(1,128)} %bitcast.13, f32[6,64]{1,0:T(8,128)} %bitcast.11, ...), custom_call_target="tpu_custom_call" | custom-call | tf_op jit(solution)/shard_map/pallas_call | solution.py:368
  103.5 0.7 copy.13
  104.2 0.6 copy.15
  104.8 0.6 copy.14

commit v4 on v3

--- a/solution.py
+++ b/solution.py
@@ -10,6 +10,8 @@
 MESH = pl.DeviceIdType.MESH
 HIGHEST = lax.Precision.HIGHEST
 ITERS = 3
+LEVELS = 32767.0
+STEPS = 32000.0
 CHUNKS = 3
 HOMES = 32
 ROWS = 64
@@ -33,8 +35,8 @@
 def kernel(
     w_hbm, moduli_hbm, fraction_hbm, plastic_hbm, id_hbm, strain_hbm, state_hbm,
     home_ref, hom_ref, res_ref,
-    w, moduli_ref, fraction_ref, plastic_ref, id_ref, strain_ref, state_ref, acc, g, tx, rx, ty, ry, tg, ebuf, pacc, px, rt, rr, st, sn,
-    w_sem, i_sem, in_send, in_recv, ag_send, ag_recv, out_send, out_recv, p_send, p_recv, r_send, r_recv, s_send, s_recv,
+    w, moduli_ref, fraction_ref, plastic_ref, id_ref, strain_ref, state_ref, acc, g, tx, rx, ty, ry, ty16, ry16, tx16, rx16, tm, rm, tg, ebuf, pacc, px, rt, rr, st, sn,
+    w_sem, i_sem, in_send, in_recv, ag_send, ag_recv, out_send, out_recv, p_send, p_recv, r_send, r_recv, m_send, m_recv, s_send, s_recv,
 ):
     micro, me = lax.axis_index("micro"), lax.axis_index("macro")
     x, r = micro // 2, micro % 2
@@ -90,20 +92,38 @@
     st[...] = jnp.concatenate([slot_row[0:8], jnp.full((8, 64), -1, jnp.int32)], axis=1)
 
     strain_cols = jnp.concatenate([strain_ref[...], jnp.zeros((122, 64), jnp.float32)], axis=0)
-    for c in range(CHUNKS):
+    peak = jnp.abs(state_ref[0])
+    for b in range(1, 6):
+        peak = jnp.maximum(peak, jnp.abs(state_ref[b]))
+    peak = jnp.maximum(jnp.max(peak, axis=1, keepdims=True), 1e-30)
+    power = jnp.ceil(jnp.log2(peak))
+    code = STEPS * jnp.exp2(-power)
+    for b in range(6):
+        state_ref[b] = jnp.round(state_ref[b] * code)
+    power = jnp.broadcast_to(power, (64, 128))
+
+    def fill(c):
         pick = jnp.where(down + c * 64 == slot_row, 1.0, 0.0)
-        for b in range(6):
-            rows = jnp.dot(pick, state_ref[b], precision=HIGHEST, preferred_element_type=jnp.float32)
+        for b in range(7):
+            rows = jnp.dot(
+                pick, state_ref[b] if b < 6 else power, precision=HIGHEST, preferred_element_type=jnp.float32
+            )
             for q in range(2):
-                tx[c, pl.ds(b * 2 + q, HOMES, stride=MSG), :] = rows[q * 32 : (q + 1) * 32]
+                tx[c, pl.ds((b * 2 if b < 6 else 14) + q, HOMES, stride=MSG), :] = rows[q * 32 : (q + 1) * 32]
         rows = lax.dot_general(
             pick, strain_cols, (((1,), (1,)), ((), ())), precision=HIGHEST, preferred_element_type=jnp.float32
         )
         for q in range(2):
-            tx[c, pl.ds(12 + q, HOMES, stride=MSG), :] = rows[q * 32 : (q + 1) * 32]
-            tx[c, pl.ds(14 + q, HOMES, stride=MSG), :] = jnp.zeros((HOMES, 128), jnp.float32)
+            tm[pl.ds(c * 2 + q, HOMES, stride=8), :] = rows[q * 32 : (q + 1) * 32]
+            tx[c, pl.ds(12 + q, HOMES, stride=MSG), :] = jnp.zeros((HOMES, 128), jnp.float32)
             ty[c, pl.ds(12 + q, HOMES, stride=MSG), :] = jnp.zeros((HOMES, 128), jnp.float32)
             ty[c, pl.ds(14 + q, HOMES, stride=MSG), :] = jnp.zeros((HOMES, 128), jnp.float32)
+        tx16[c] = tx[c].astype(jnp.int32).astype(jnp.int16)
+
+    for c in range(CHUNKS):
+        fill(c)
+    for spare in (6, 7):
+        tm[pl.ds(spare, HOMES, stride=8), :] = jnp.zeros((HOMES, 128), jnp.float32)
     pacc[...] = jnp.zeros((128, 128), jnp.float32)
 
     pl.semaphore_wait(barrier, 31 + 7)
@@ -128,8 +148,25 @@
     def drain(ref, sem):
         pltpu.make_async_copy(ref, ref, sem).wait()
 
-    for c in range(CHUNKS):
-        exchange(tx, rx, c, in_send, in_recv)
+    exchange(tx16, rx16, 0, in_send, in_recv)
+
+    def aim(i, carry):
+        to = far(i)
+        pltpu.make_async_remote_copy(
+            src_ref=tm.at[pl.ds(pl.multiple_of(to * 8, 8), 8), :],
+            dst_ref=rm.at[pl.ds(pl.multiple_of(me * 8, 8), 8), :],
+            send_sem=m_send,
+            recv_sem=m_recv,
+            device_id=(micro, to),
+            device_id_type=MESH,
+        ).start()
+        return carry
+
+    lax.fori_loop(0, HOMES - 1, aim, 0)
+    own = pl.ds(pl.multiple_of(me * 8, 8), 8)
+    rm[own, :] = tm[own, :]
+    for c in range(1, CHUNKS):
+        exchange(tx16, rx16, c, in_send, in_recv)
     for side in range(2):
         pltpu.make_async_remote_copy(
             src_ref=st,
@@ -186,13 +223,15 @@
 
         @pl.when(p < CHUNKS)
         def _():
-            drain(rx.at[p, 0 : 31 * MSG], in_recv.at[p])
+            drain(rx16.at[p, 0 : 31 * MSG], in_recv.at[p])
+            rx[p] = rx16[p].astype(jnp.int32).astype(jnp.float32)
             strain = [
                 jnp.concatenate([rx[p, pl.ds(b * 2 + q, HOMES, stride=MSG), :] for q in range(2)], axis=0)
                 for b in range(6)
             ]
-            tg[p] = jnp.concatenate([rx[p, pl.ds(12 + q, HOMES, stride=MSG), :] for q in range(2)], axis=0)
-            polarize(p, strain)
+            power = jnp.concatenate([rx[p, pl.ds(14 + q, HOMES, stride=MSG), :] for q in range(2)], axis=0)
+            scale = jnp.exp2(power) * (1.0 / STEPS)
+            polarize(p, [plane * scale for plane in strain])
 
         @pl.when(p >= 2)
         def _():
@@ -218,6 +257,9 @@
             @pl.when(p == 2)
             def _():
                 load_w.wait()
+                drain(rm.at[0 : 31 * 8], m_recv)
+                for i in range(CHUNKS):
+                    tg[i] = jnp.concatenate([rm[pl.ds(i * 2 + q, HOMES, stride=8), :] for q in range(2)], axis=0)
 
             for a in range(6):
                 acc[a] = partial(s, a, [micro, left, right, across])
@@ -263,7 +305,12 @@
                 for a in range(6):
                     part = jnp.sum(stress[a] * fraction, axis=1, keepdims=True)
                     sums = jnp.where(lane == c * 8 + a, part, sums)
-                pacc[0:ROWS] = sums
+                peak = jnp.abs(strain[0])
+                for a in range(1, 6):
+                    peak = jnp.maximum(peak, jnp.abs(strain[a]))
+                peak = jnp.maximum(jnp.max(peak, axis=1, keepdims=True), 1e-30)
+                pacc[0:ROWS] = jnp.where(lane == c * 8 + 7, peak, sums)
+                code = LEVELS / peak
 
                 @pl.when(s == STAGES - 1)
                 def _():
@@ -274,8 +321,10 @@
 
                 for b in range(6):
                     for q in range(2):
-                        ty[c, pl.ds(b * 2 + q, HOMES, stride=MSG), :] = ebuf[b, q * 32 : (q + 1) * 32]
-                exchange(ty, ry, c, out_send, out_recv)
+                        half = slice(q * 32, (q + 1) * 32)
+                        ty[c, pl.ds(b * 2 + q, HOMES, stride=MSG), :] = strain[b][half] * code[half]
+                ty16[c] = jnp.round(ty[c]).astype(jnp.int32).astype(jnp.int16)
+                exchange(ty16, ry16, c, out_send, out_recv)
 
         return carry
 
@@ -285,7 +334,8 @@
     sums = px[0]
     for i in range(1, 8):
         sums = sums + px[i]
-    mean = sums / sums[6:7]
+    row = lax.broadcasted_iota(jnp.int32, (8 * CHUNKS, 128), 0)
+    mean = jnp.where(row % 8 == 7, px[micro], sums / sums[6:7])
     mean = jnp.concatenate([mean, jnp.zeros((128 - 8 * CHUNKS, 128), jnp.float32)], axis=0).T
     for d in range(3):
         for q in range(2):
@@ -313,7 +363,8 @@
     rr[own, :] = rt[own, :]
 
     for c in range(CHUNKS):
-        drain(ry.at[c, 0 : 31 * MSG], out_recv.at[c])
+        drain(ry16.at[c, 0 : 31 * MSG], out_recv.at[c])
+        ry[c] = ry16[c].astype(jnp.int32).astype(jnp.float32)
         pick = jnp.where(along + c * 64 == slot_col, 1.0, 0.0)
         for b in range(6):
             rows = jnp.concatenate([ry[c, pl.ds(b * 2 + q, HOMES, stride=MSG), :] for q in range(2)], axis=0)
@@ -323,6 +374,15 @@
     for side in range(2):
         drain(sn.at[side], s_recv.at[side])
     drain(rr.at[0 : 31 * 8], r_recv)
+    peaks = jnp.concatenate([rr[pl.ds(2 + q, HOMES, stride=8), :] for q in range(2)], axis=0)
+    scale = jnp.zeros((64, 1), jnp.float32)
+    for c in range(CHUNKS):
+        pick = jnp.where(along + c * 64 == slot_col, 1.0, 0.0)
+        found = jnp.dot(pick, peaks, precision=HIGHEST, preferred_element_type=jnp.float32)
+        scale = scale + found[:, c * 8 + 7 : c * 8 + 8]
+    scale = scale * (1.0 / LEVELS)
+    for b in range(6):
+        home_ref[b] = home_ref[b] * scale
     slots = [sn[0][0:1], st[0:1], sn[1][0:1]]
     down2 = lax.broadcasted_iota(jnp.int32, (64, 128), 0)
     hom = []
@@ -349,8 +409,8 @@
     res_ref[...] = jnp.concatenate([res_x, res_y, res_z], axis=0)[:, 0:64]
 
     for c in range(CHUNKS):
-        drain(tx.at[c, 0 : 31 * MSG], in_send.at[c])
-        drain(ty.at[c, 0 : 31 * MSG], out_send.at[c])
+        drain(tx16.at[c, 0 : 31 * MSG], in_send.at[c])
+        drain(ty16.at[c, 0 : 31 * MSG], out_send.at[c])
     for side in range(2):
         drain(st, s_send.at[side])
 
@@ -360,6 +420,7 @@
 
     lax.fori_loop(0, STAGES, sent, 0)
     drain(px.at[0:7], p_send)
+    drain(tm.at[0 : 31 * 8], m_send)
     drain(rt.at[0 : 31 * 8], r_send)
 
 
@@ -388,6 +449,12 @@
             pltpu.VMEM((CHUNKS, HOMES * MSG, 128), jnp.float32),
             pltpu.VMEM((CHUNKS, HOMES * MSG, 128), jnp.float32),
             pltpu.VMEM((CHUNKS, HOMES * MSG, 128), jnp.float32),
+            pltpu.VMEM((CHUNKS, HOMES * MSG, 128), jnp.int16),
+            pltpu.VMEM((CHUNKS, HOMES * MSG, 128), jnp.int16),
+            pltpu.VMEM((CHUNKS, HOMES * MSG, 128), jnp.int16),
+            pltpu.VMEM((CHUNKS, HOMES * MSG, 128), jnp.int16),
+            pltpu.VMEM((HOMES * 8, 128), jnp.float32),
+            pltpu.VMEM((HOMES * 8, 128), jnp.float32),
             pltpu.VMEM((CHUNKS, ROWS, 128), jnp.float32),
             pltpu.VMEM((6, ROWS, 128), jnp.float32),
             pltpu.VMEM((128, 128), jnp.float32),
@@ -404,6 +471,8 @@
             pltpu.SemaphoreType.DMA((STAGES, 6)),
             pltpu.SemaphoreType.DMA((CHUNKS,)),
             pltpu.SemaphoreType.DMA((CHUNKS,)),
+            pltpu.SemaphoreType.DMA,
+            pltpu.SemaphoreType.DMA,
             pltpu.SemaphoreType.DMA,
             pltpu.SemaphoreType.DMA,
             pltpu.SemaphoreType.DMA,

time: 105 us -> 101 us (0.962)
  Pallas kernels: 103 us -> 98 us
    pallas_call x1, Pallas kernels: 103 us -> 98 us  [local(): pl.pallas_call(kernel, out_shape=(pltpu.VMEM((6, 64, 128), jnp.float32),...]
where the time goes in v4:
time: 101 us
  Pallas kernels  98 us (97%)
  local copies, waits for them, and re-layouts  1.85 us (2%)
    pallas_call x1, Pallas kernels, local(): pl.pallas_call(kernel, out_shape=(pltpu.VMEM((6, 64, 128), jnp.float32),...  98 us

profile of v4, /device:TPU:1, one launch (start us, length us, event | category | flops | bytes accessed | tf_op | source)
XLA Modules:
  0.0 100.5 jit_solution(11818295349467085913)
XLA Ops:
  0.6 98.0 %shard_map.94 = (f32[6,64,128]{2,1,0:T(8,128)S(1)}, f32[6,64]{1,0:T(8,128)S(1)}, f32[3,64]{1,0:T(4,128)S(1)}) custom-call(bf16[6,6,128,1024]{3,2,1,0:T(8,128)(2,1)} %bitcast.9, f32[3,1,128]{2,1,0:T(1,128)} %bitcast.12, f32[1,128]{1,0:T(1,128)} %fraction_hbm.1, s32[1,128]{1,0:T(1,128)} %plastic_hbm.1, s32[1,64]{1,0:T(1,128)} %bitcast.13, f32[6,64]{1,0:T(8,128)} %bitcast.11, ...), custom_call_target="tpu_custom_call" | custom-call | tf_op jit(solution)/shard_map/pallas_call | solution.py:429
  98.7 0.7 copy.13
  99.3 0.6 copy.15
  99.9 0.6 copy.14

commit v5 on v3

--- a/solution.py
+++ b/solution.py
@@ -10,6 +10,7 @@
 MESH = pl.DeviceIdType.MESH
 HIGHEST = lax.Precision.HIGHEST
 ITERS = 3
+LEVELS = 32767.0
 CHUNKS = 3
 HOMES = 32
 ROWS = 64
@@ -33,7 +34,7 @@
 def kernel(
     w_hbm, moduli_hbm, fraction_hbm, plastic_hbm, id_hbm, strain_hbm, state_hbm,
     home_ref, hom_ref, res_ref,
-    w, moduli_ref, fraction_ref, plastic_ref, id_ref, strain_ref, state_ref, acc, g, tx, rx, ty, ry, tg, ebuf, pacc, px, rt, rr, st, sn,
+    w, moduli_ref, fraction_ref, plastic_ref, id_ref, strain_ref, state_ref, acc, g, tx, rx, ty, ry, ty16, ry16, tg, ebuf, pacc, px, rt, rr, st, sn,
     w_sem, i_sem, in_send, in_recv, ag_send, ag_recv, out_send, out_recv, p_send, p_recv, r_send, r_recv, s_send, s_recv,
 ):
     micro, me = lax.axis_index("micro"), lax.axis_index("macro")
@@ -90,7 +91,7 @@
     st[...] = jnp.concatenate([slot_row[0:8], jnp.full((8, 64), -1, jnp.int32)], axis=1)
 
     strain_cols = jnp.concatenate([strain_ref[...], jnp.zeros((122, 64), jnp.float32)], axis=0)
-    for c in range(CHUNKS):
+    def fill(c):
         pick = jnp.where(down + c * 64 == slot_row, 1.0, 0.0)
         for b in range(6):
             rows = jnp.dot(pick, state_ref[b], precision=HIGHEST, preferred_element_type=jnp.float32)
@@ -104,6 +105,8 @@
             tx[c, pl.ds(14 + q, HOMES, stride=MSG), :] = jnp.zeros((HOMES, 128), jnp.float32)
             ty[c, pl.ds(12 + q, HOMES, stride=MSG), :] = jnp.zeros((HOMES, 128), jnp.float32)
             ty[c, pl.ds(14 + q, HOMES, stride=MSG), :] = jnp.zeros((HOMES, 128), jnp.float32)
+
+    fill(0)
     pacc[...] = jnp.zeros((128, 128), jnp.float32)
 
     pl.semaphore_wait(barrier, 31 + 7)
@@ -128,7 +131,9 @@
     def drain(ref, sem):
         pltpu.make_async_copy(ref, ref, sem).wait()
 
-    for c in range(CHUNKS):
+    exchange(tx, rx, 0, in_send, in_recv)
+    for c in range(1, CHUNKS):
+        fill(c)
         exchange(tx, rx, c, in_send, in_recv)
     for side in range(2):
         pltpu.make_async_remote_copy(
@@ -263,7 +268,12 @@
                 for a in range(6):
                     part = jnp.sum(stress[a] * fraction, axis=1, keepdims=True)
                     sums = jnp.where(lane == c * 8 + a, part, sums)
-                pacc[0:ROWS] = sums
+                peak = jnp.abs(strain[0])
+                for a in range(1, 6):
+                    peak = jnp.maximum(peak, jnp.abs(strain[a]))
+                peak = jnp.maximum(jnp.max(peak, axis=1, keepdims=True), 1e-30)
+                pacc[0:ROWS] = jnp.where(lane == c * 8 + 7, peak, sums)
+                code = LEVELS / peak
 
                 @pl.when(s == STAGES - 1)
                 def _():
@@ -274,8 +284,10 @@
 
                 for b in range(6):
                     for q in range(2):
-                        ty[c, pl.ds(b * 2 + q, HOMES, stride=MSG), :] = ebuf[b, q * 32 : (q + 1) * 32]
-                exchange(ty, ry, c, out_send, out_recv)
+                        half = slice(q * 32, (q + 1) * 32)
+                        ty[c, pl.ds(b * 2 + q, HOMES, stride=MSG), :] = strain[b][half] * code[half]
+                ty16[c] = jnp.round(ty[c]).astype(jnp.int32).astype(jnp.int16)
+                exchange(ty16, ry16, c, out_send, out_recv)
 
         return carry
 
@@ -285,7 +297,8 @@
     sums = px[0]
     for i in range(1, 8):
         sums = sums + px[i]
-    mean = sums / sums[6:7]
+    row = lax.broadcasted_iota(jnp.int32, (8 * CHUNKS, 128), 0)
+    mean = jnp.where(row % 8 == 7, px[micro], sums / sums[6:7])
     mean = jnp.concatenate([mean, jnp.zeros((128 - 8 * CHUNKS, 128), jnp.float32)], axis=0).T
     for d in range(3):
         for q in range(2):
@@ -313,7 +326,8 @@
     rr[own, :] = rt[own, :]
 
     for c in range(CHUNKS):
-        drain(ry.at[c, 0 : 31 * MSG], out_recv.at[c])
+        drain(ry16.at[c, 0 : 31 * MSG], out_recv.at[c])
+        ry[c] = ry16[c].astype(jnp.int32).astype(jnp.float32)
         pick = jnp.where(along + c * 64 == slot_col, 1.0, 0.0)
         for b in range(6):
             rows = jnp.concatenate([ry[c, pl.ds(b * 2 + q, HOMES, stride=MSG), :] for q in range(2)], axis=0)
@@ -323,6 +337,15 @@
     for side in range(2):
         drain(sn.at[side], s_recv.at[side])
     drain(rr.at[0 : 31 * 8], r_recv)
+    peaks = jnp.concatenate([rr[pl.ds(2 + q, HOMES, stride=8), :] for q in range(2)], axis=0)
+    scale = jnp.zeros((64, 1), jnp.float32)
+    for c in range(CHUNKS):
+        pick = jnp.where(along + c * 64 == slot_col, 1.0, 0.0)
+        found = jnp.dot(pick, peaks, precision=HIGHEST, preferred_element_type=jnp.float32)
+        scale = scale + found[:, c * 8 + 7 : c * 8 + 8]
+    scale = scale * (1.0 / LEVELS)
+    for b in range(6):
+        home_ref[b] = home_ref[b] * scale
     slots = [sn[0][0:1], st[0:1], sn[1][0:1]]
     down2 = lax.broadcasted_iota(jnp.int32, (64, 128), 0)
     hom = []
@@ -350,7 +373,7 @@
 
     for c in range(CHUNKS):
         drain(tx.at[c, 0 : 31 * MSG], in_send.at[c])
-        drain(ty.at[c, 0 : 31 * MSG], out_send.at[c])
+        drain(ty16.at[c, 0 : 31 * MSG], out_send.at[c])
     for side in range(2):
         drain(st, s_send.at[side])
 
@@ -388,6 +411,8 @@
             pltpu.VMEM((CHUNKS, HOMES * MSG, 128), jnp.float32),
             pltpu.VMEM((CHUNKS, HOMES * MSG, 128), jnp.float32),
             pltpu.VMEM((CHUNKS, HOMES * MSG, 128), jnp.float32),
+            pltpu.VMEM((CHUNKS, HOMES * MSG, 128), jnp.int16),
+            pltpu.VMEM((CHUNKS, HOMES * MSG, 128), jnp.int16),
             pltpu.VMEM((CHUNKS, ROWS, 128), jnp.float32),
             pltpu.VMEM((6, ROWS, 128), jnp.float32),
             pltpu.VMEM((128, 128), jnp.float32),

time: 105 us -> 105 us (level)
  no operation moved by 1% of the time
where the time goes in v5:
time: 105 us; the launch traced here: 104 us
  Pallas kernels  102 us (97%)
  local copies, waits for them, and re-layouts  1.85 us (2%)
    pallas_call x1, Pallas kernels, local(): pl.pallas_call(kernel, out_shape=(pltpu.VMEM((6, 64, 128), jnp.float32),...  102 us

profile of v5, /device:TPU:1, one launch (start us, length us, event | category | flops | bytes accessed | tf_op | source)
XLA Modules:
  0.0 104.5 jit_solution(5878134868339434802)
XLA Ops:
  0.6 102.0 %shard_map.94 = (f32[6,64,128]{2,1,0:T(8,128)S(1)}, f32[6,64]{1,0:T(8,128)S(1)}, f32[3,64]{1,0:T(4,128)S(1)}) custom-call(bf16[6,6,128,1024]{3,2,1,0:T(8,128)(2,1)} %bitcast.9, f32[3,1,128]{2,1,0:T(1,128)} %bitcast.12, f32[1,128]{1,0:T(1,128)} %fraction_hbm.1, s32[1,128]{1,0:T(1,128)} %plastic_hbm.1, s32[1,64]{1,0:T(1,128)} %bitcast.13, f32[6,64]{1,0:T(8,128)} %bitcast.11, ...), custom_call_target="tpu_custom_call" | custom-call | tf_op jit(solution)/shard_map/pallas_call | solution.py:391
  102.6 0.7 copy.13
  103.3 0.6 copy.15
  103.9 0.6 copy.14
